TPU v7x, 512 devices: a whole 4x4x16 slice. The times are simulated.
512 devices in a mesh: row: 16 (over x, y_lo, core), col: 32 (over z, y_hi).
Axes of the slice: x: 4, y: 4 (y_hi: 2, y_lo: 2; y = y_hi * 2 + y_lo), z: 16, core: 2. Of those that a mesh axis runs over, the one named last changes fastest.
Arguments:
- features: bfloat16 [128, 1024, 256], P('row', 'col'), may hold values from -16 to 16
- expand_weight: bfloat16 [2, 256, 1024], replicated, may hold values from -0.375 to 0.375
- expand_bias: float32 [2, 1024], replicated, may hold values from -3 to 3
- depth_weight: float32 [2, 3, 3, 1024], replicated, may hold values from -2 to 2
- depth_bias: float32 [2, 1024], replicated, may hold values from -3 to 3
- project_weight: bfloat16 [2, 1024, 256], replicated, may hold values from -0.1875 to 0.1875
- project_bias: float32 [2, 256], replicated, may hold values from -3 to 3
- qkv_weight: bfloat16 [2, 256, 768], replicated, may hold values from -0.375 to 0.375
- aggregate_depth: float32 [2, 5, 5, 768], replicated, may hold values from -1.25 to 1.25
- aggregate_group: bfloat16 [2, 24, 32, 32], replicated, may hold values from -1 to 1
- output_weight: bfloat16 [2, 512, 256], replicated, may hold values from -0.25 to 0.25
- output_bias: float32 [2, 256], replicated, may hold values from -3 to 3
- head_weight: bfloat16 [3, 3, 4, 256], replicated, may hold values from -0.125 to 0.125
- head_bias: float32 [4], replicated, may hold values from -3 to 3
Outputs:
- final_map: bfloat16 [128, 1024, 256], P('row', 'col')
- boxes: float32 [4, 128, 1024], P(None, 'row', 'col')
All inputs are finite; a program needn't handle non-finite values.
Results may differ from a plain program's by a relative error of at most 0.009.
Values may be sent and summed in bfloat16 or wider, within the bound.
A program may use at most 64 MiB of HBM per device.

v0:
```python
import jax
import jax.numpy as jnp
from jax import lax
from jax.sharding import PartitionSpec as P

SECTIONS = 2


def with_halo(cells, sides, width):
    for axis, dim in sides:
        count = lax.axis_size(axis)
        ends = count - 1
        head = lax.slice_in_dim(cells, 0, width, axis=dim)
        tail = lax.slice_in_dim(cells, cells.shape[dim] - width, cells.shape[dim], axis=dim)
        cells = jnp.concatenate(
            [
                lax.ppermute(tail, axis, [(i, (i + 1) % count) for i in range(ends)]),
                cells,
                lax.ppermute(head, axis, [((i + 1) % count, i) for i in range(ends)]),
            ],
            axis=dim,
        )
    return cells


def hard_swish(value):
    return value * jnp.minimum(jnp.maximum(value + 3.0, 0.0), 6.0) / 6.0


def depthwise(padded, weight, rows, cols):
    ksize = weight.shape[0]
    total = jnp.zeros((rows, cols, padded.shape[2]), jnp.float32)
    for offset_r in range(ksize):
        for offset_c in range(ksize):
            total = (
                total
                + padded[offset_r : offset_r + rows, offset_c : offset_c + cols, :].astype(
                    jnp.float32
                )
                * weight[offset_r, offset_c]
            )
    return total


def dense(values, weight):
    return lax.dot_general(
        values, weight, (((values.ndim - 1,), (0,)), ((), ())), preferred_element_type=jnp.float32
    )


def heads_of(padded_qkv, agg_depth, agg_group, rows, cols, heads, head_dim):
    center = padded_qkv[2 : 2 + rows, 2 : 2 + cols, :]
    spread = depthwise(padded_qkv, agg_depth, rows, cols).astype(jnp.bfloat16)
    grouped = jnp.einsum(
        "rcgd,gde->rcge",
        spread.reshape(rows, cols, 3 * heads, head_dim),
        agg_group,
        preferred_element_type=jnp.float32,
    ).astype(jnp.bfloat16)
    return jnp.concatenate(
        [
            center.reshape(rows, cols, heads, 3, head_dim),
            grouped.reshape(rows, cols, heads, 3, head_dim),
        ],
        axis=2,
    )


def local(
    features,
    expand_weight,
    expand_bias,
    depth_weight,
    depth_bias,
    project_weight,
    project_bias,
    qkv_weight,
    aggregate_depth,
    aggregate_group,
    output_weight,
    output_bias,
    head_weight,
    head_bias,
):
    rows, cols, width = features.shape
    head_dim = aggregate_group.shape[2]
    heads = width // head_dim
    current = features
    for section in range(SECTIONS):
        hidden = hard_swish(dense(current, expand_weight[section]) + expand_bias[section]).astype(
            jnp.bfloat16
        )
        hidden = with_halo(hidden, (("row", 0), ("col", 1)), 1)
        spread = hard_swish(
            depthwise(hidden, depth_weight[section], rows, cols) + depth_bias[section]
        ).astype(jnp.bfloat16)
        mixed = (current + dense(spread, project_weight[section]) + project_bias[section]).astype(
            jnp.bfloat16
        )
        local_qkv = dense(mixed, qkv_weight[section]).astype(jnp.bfloat16)
        padded_qkv = with_halo(local_qkv, (("row", 0), ("col", 1)), 2)
        both = heads_of(
            padded_qkv,
            aggregate_depth[section],
            aggregate_group[section],
            rows,
            cols,
            heads,
            head_dim,
        )
        queries = jax.nn.relu(both[:, :, :, 0, :]).astype(jnp.float32)
        keys = jax.nn.relu(both[:, :, :, 1, :]).astype(jnp.float32)
        values = both[:, :, :, 2, :].astype(jnp.float32)
        kv_local = jnp.einsum("rchd,rche->hde", keys, values, precision=lax.Precision.HIGHEST)
        key_local = jnp.sum(keys, axis=(0, 1))
        kv_all, key_all = lax.psum((kv_local, key_local), ("row", "col"))
        numer = jnp.einsum("rchd,hde->rche", queries, kv_all, precision=lax.Precision.HIGHEST)
        denom = jnp.einsum("rchd,hd->rch", queries, key_all, precision=lax.Precision.HIGHEST)
        attended = (
            (numer / (denom[..., None] + 1e-06)).astype(jnp.bfloat16).reshape(rows, cols, 2 * width)
        )
        current = (mixed + dense(attended, output_weight[section]) + output_bias[section]).astype(
            jnp.bfloat16
        )
    padded = with_halo(current, (("row", 0), ("col", 1)), 1)
    boxes = jnp.zeros((4, rows, cols), jnp.float32)
    for offset_r in range(3):
        for offset_c in range(3):
            window = padded[offset_r : offset_r + rows, offset_c : offset_c + cols, :]
            boxes = boxes + lax.dot_general(
                head_weight[offset_r, offset_c],
                window,
                (((1,), (2,)), ((), ())),
                preferred_element_type=jnp.float32,
            )
    boxes = boxes + head_bias[:, None, None]
    return (current, boxes)


def solution(mesh):
    return jax.shard_map(
        local,
        mesh=mesh,
        in_specs=(
            P("row", "col", None),
            P(),
            P(),
            P(),
            P(),
            P(),
            P(),
            P(),
            P(),
            P(),
            P(),
            P(),
            P(),
            P(),
        ),
        out_specs=(P("row", "col", None), P(None, "row", "col")),
        check_vma=False,
    )
```

profile of v0, /device:TPU:1, one launch (start us, length us, event | category | flops | bytes accessed | tf_op | source)
XLA Modules:
  0.0 1291.3 jit_solution(16654592046291332820)
XLA Ops:
  10.1 4.6 collective-permute-start
  14.7 5.5 collective-permute-start.1
  27.0 4.2 collective-permute-done.3
  34.1 3.7 collective-permute-start.4
  42.0 2.0 collective-permute-done.5
  44.0 6.0 collective-permute-start.6
  53.3 2.9 collective-permute-done.7
  56.7 3.0 add_convert_fusion.1
  66.0 111.1 %psum.29 = f32[16,32]{1,0:T(8,128)S(1)} all-reduce(f32[16,32]{1,0:T(8,128)S(1)} %convert_reduce_fusion.1), channel_id=1, replica_groups=mesh['row'=16,'col'=32] {'row','col'}, use_global_device_ids=true, to_apply=%region_2.3 | all-reduce | flops 512 | bytes 4096 | tf_op jit(solution)/shard_map/psum | solution.py:116
  177.0 5.4 fusion.26
  182.5 450.1 %all-reduce.3.cloned.1.call-done = f32[16,32,32]{1,2,0:T(8,128)} async-done(((f32[16,32,32]{1,2,0:T(8,128)}), f32[16,32,32]{1,2,0:T(8,128)}) %all-reduce.3.cloned.1.call-update) | async-done | bytes 65552 | tf_op jit(solution)/shard_map/psum | solution.py:116
  632.6 6.1 fusion.1
  642.4 4.9 collective-permute-start.8
  647.3 1.9 collective-permute-start.9
  649.3 3.6 collective-permute-done.9
  653.0 4.5 collective-permute-start.10
  658.9 4.8 collective-permute-done.11
  666.0 2.7 collective-permute-start.12
  668.7 1.9 collective-permute-start.13
  672.3 2.3 collective-permute-done.13
  674.7 3.1 collective-permute-start.14
  681.2 2.8 collective-permute-done.15
  684.3 3.0 add_convert_fusion
  693.6 105.8 %psum.31 = f32[16,32]{1,0:T(8,128)S(1)} all-reduce(f32[16,32]{1,0:T(8,128)S(1)} %convert_reduce_fusion), channel_id=1, replica_groups=mesh['row'=16,'col'=32] {'row','col'}, use_global_device_ids=true, to_apply=%region_5.6 | all-reduce | flops 512 | bytes 4096 | tf_op jit(solution)/shard_map/psum | solution.py:116
  799.4 5.4 fusion.29
  804.9 448.7 %all-reduce.5.cloned.1.call-done = f32[16,32,32]{1,2,0:T(8,128)} async-done(((f32[16,32,32]{1,2,0:T(8,128)}), f32[16,32,32]{1,2,0:T(8,128)}) %all-reduce.5.cloned.1.call-update) | async-done | bytes 65552 | tf_op jit(solution)/shard_map/psum | solution.py:116
  1253.6 6.1 fusion
  1262.1 4.9 collective-permute-start.16
  1267.0 1.9 collective-permute-start.17
  1269.2 2.9 collective-permute-done.17
  1272.1 4.5 collective-permute-start.18
  1278.3 4.2 collective-permute-done.19
  (183 shorter events, 51.5 us)
Async XLA Ops:
  7.2 13.7 %copy-start.32 = (f32[2,1024]{1,0:T(2,128)S(1)}, f32[2,1024]{1,0:T(2,128)}, u32[]{:S(2)}) copy-start(f32[2,1024]{1,0:T(2,128)} %param.18) | copy-start | bytes 24580
  7.2 14.3 %copy-start.14 = (f32[2,3,3,1024]{3,0,2,1:T(2,128)S(1)}, f32[2,3,3,1024]{3,0,2,1:T(2,128)}, u32[]{:S(2)}) copy-start(f32[2,3,3,1024]{3,0,2,1:T(2,128)} %param.17) | copy-start | bytes 221188
  7.2 14.4 %copy-start.9 = (f32[2,5,5,768]{3,0,2,1:T(2,128)S(1)}, f32[2,5,5,768]{3,0,2,1:T(2,128)}, u32[]{:S(2)}) copy-start(f32[2,5,5,768]{3,0,2,1:T(2,128)} %param.22) | copy-start | bytes 460804
  7.2 625.4 %all-reduce.3.cloned.1.call-start = ((), (), s32[]{:S(2)}) async-start(), calls=%async_computation | async-start | bytes 524288 | tf_op jit(solution)/shard_map/psum | solution.py:116
  8.6 13.8 %copy-start.36 = (f32[2,256]{1,0:T(2,128)S(1)}, f32[2,256]{1,0:T(2,128)}, u32[]{:S(2)}) copy-start(f32[2,256]{1,0:T(2,128)} %param.25) | copy-start | bytes 6148
  10.1 12.8 collective-permute-start
  14.7 8.2 collective-permute-start.1
  23.1 3.9 collective-permute-start.2
  24.9 6.3 collective-permute-start.3
  34.1 7.9 collective-permute-start.4
  37.8 6.1 collective-permute-start.5
  44.0 9.3 collective-permute-start.6
  50.0 6.2 collective-permute-start.7
  182.4 1071.2 %all-reduce.5.cloned.1.call-start = ((), (), s32[]{:S(2)}) async-start(), calls=%async_computation.1 | async-start | bytes 524288 | tf_op jit(solution)/shard_map/psum | solution.py:116
  642.0 16.8 %copy-start.8 = (f32[5,5,768]{2,1,0:T(8,128)S(1)}, f32[5,5,768]{2,1,0:T(8,128)}, u32[]{:S(2)}) copy-start(f32[5,5,768]{2,1,0:T(8,128)} %get-tuple-element.118) | copy-start | bytes 230404
  642.4 7.0 collective-permute-start.8
  647.3 5.6 collective-permute-start.9
  649.3 14.8 %copy-start.33 = (f32[1,1024]{1,0:T(1,128)S(1)}, f32[1,1024]{1,0:T(1,128)}, u32[]{:S(2)}) copy-start(f32[1,1024]{1,0:T(1,128)} %get-tuple-element.108) | copy-start | bytes 12292
  649.3 14.8 %copy-start.38 = (f32[1,256]{1,0:T(1,128)S(1)}, f32[1,256]{1,0:T(1,128)}, u32[]{:S(2)}) copy-start(f32[1,256]{1,0:T(1,128)} %get-tuple-element.114) | copy-start | bytes 3076
  649.3 14.8 %copy-start.43 = (bf16[2,1024,256]{2,1,0:T(8,128)(2,1)S(1)}, bf16[2,1024,256]{2,1,0:T(8,128)(2,1)}, u32[]{:S(2)}) copy-start(bf16[2,1024,256]{2,1,0:T(8,128)(2,1)} %param.19) | copy-start | bytes 3145732
  653.0 6.0 collective-permute-start.10
  657.5 6.3 collective-permute-start.11
  666.0 6.3 collective-permute-start.12
  668.7 5.9 collective-permute-start.13
  674.7 6.6 collective-permute-start.14
  677.8 6.2 collective-permute-start.15
  1261.8 21.8 %copy-start.46 = (f32[4]{0:T(128)S(1)}, f32[4]{0:T(128)}, u32[]{:S(2)}) copy-start(f32[4]{0:T(128)} %param.27) | copy-start | bytes 52
  1262.0 22.4 %copy-start.4 = (bf16[8,32,256]{2,1,0:T(8,128)(2,1)}, bf16[8,32,256]{2,1,0:T(8,128)(2,1)S(1)}, u32[]{:S(2)}) copy-start(bf16[8,32,256]{2,1,0:T(8,128)(2,1)S(1)} %fusion.9) | copy-start | bytes 393220
  1262.1 7.1 collective-permute-start.16
  1267.0 5.1 collective-permute-start.17
  1272.1 6.2 collective-permute-start.18
  1276.6 5.9 collective-permute-start.19
  (37 other events, 134.4 us)
Sparse Core Ops, SparseCore 0:
  182.6 449.9 all-reduce.2
  805.0 448.5 all-reduce.4
where the time goes:
time: 1290 us
  waiting for transfers between devices  929 us (72%)
  blocking collectives  217 us (17%)
  starting transfers between devices  60.7 us (5%)
  matrix products  35 us (3%)
  local copies, waits for them, and re-layouts  26.6 us (2%)
  between operations  15.2 us (1%)
    psum x2, waiting for transfers between devices, local(): kv_all, key_all = lax.psum((kv_local, key_local), ('row', 'col'))  899 us
    psum x2, blocking collectives, local(): kv_all, key_all = lax.psum((kv_local, key_local), ('row', 'col'))  217 us
    ppermute x10, starting transfers between devices, with_halo(): lax.ppermute(tail, axis, [(i, (i + 1) % count) for i in range(ends)])  40.8 us
    ppermute x10, waiting for transfers between devices, with_halo(): lax.ppermute(head, axis, [((i + 1) % count, i) for i in range(ends)])  29.7 us
  transfers between devices with their start and end apart: 22, of which 11 were waited for; matrix products, arithmetic and copies ran while one was open for 1% of the time, Pallas kernels for 0%

commit v1 on v0

--- a/solution.py
+++ b/solution.py
@@ -113,7 +113,15 @@
         values = both[:, :, :, 2, :].astype(jnp.float32)
         kv_local = jnp.einsum("rchd,rche->hde", keys, values, precision=lax.Precision.HIGHEST)
         key_local = jnp.sum(keys, axis=(0, 1))
-        kv_all, key_all = lax.psum((kv_local, key_local), ("row", "col"))
+
+        def fill_weights(x_part):
+            chip_axis = "row"
+            comm_axis = "col"
+            for src_i in (comm_axis, chip_axis):
+                x_part = lax.psum(x_part, axis_name=src_i)
+            return x_part
+
+        kv_all, key_all = fill_weights((kv_local, key_local))
         numer = jnp.einsum("rchd,hde->rche", queries, kv_all, precision=lax.Precision.HIGHEST)
         denom = jnp.einsum("rchd,hd->rch", queries, key_all, precision=lax.Precision.HIGHEST)
         attended = (

time: 1290 us -> 1240 us (0.961)
  waiting for transfers between devices: 929 us -> 883 us
    psum x2 -> x4, waiting for transfers between devices: 899 us -> 855 us  [fill_weights(): x_part = lax.psum(x_part, axis_name=src_i)]
    psum x2 -> x4, blocking collectives: 217 us -> 211 us  [fill_weights(): x_part = lax.psum(x_part, axis_name=src_i)]
  transfers between devices with their start and end apart: 22 -> 24, of which waited for: 11 -> 13; matrix products, arithmetic and copies ran while one was open for 1% -> 2% of each run, Pallas kernels for 0% -> 0%
where the time goes in v1:
time: 1240 us
  waiting for transfers between devices  883 us (71%)
  blocking collectives  211 us (17%)
  starting transfers between devices  58.8 us (5%)
  matrix products  35 us (3%)
  local copies, waits for them, and re-layouts  26.6 us (2%)
  between operations  15 us (1%)
    psum x4, waiting for transfers between devices, fill_weights(): x_part = lax.psum(x_part, axis_name=src_i)  855 us
    psum x4, blocking collectives, fill_weights(): x_part = lax.psum(x_part, axis_name=src_i)  211 us
    ppermute x10, starting transfers between devices, with_halo(): lax.ppermute(tail, axis, [(i, (i + 1) % count) for i in range(ends)])  36.9 us
    ppermute x10, waiting for transfers between devices, with_halo(): lax.ppermute(head, axis, [((i + 1) % count, i) for i in range(ends)])  28.3 us
  transfers between devices with their start and end apart: 24, of which 13 were waited for; matrix products, arithmetic and copies ran while one was open for 2% of the time, Pallas kernels for 0%

profile of v1, /device:TPU:1, one launch (start us, length us, event | category | flops | bytes accessed | tf_op | source)
XLA Modules:
  0.0 1238.3 jit_solution(15530430636415531474)
XLA Ops:
  10.1 4.6 collective-permute-start
  14.7 5.5 collective-permute-start.1
  27.0 4.2 collective-permute-done.3
  34.1 3.7 collective-permute-start.4
  44.0 6.0 collective-permute-start.6
  53.3 2.9 collective-permute-done.7
  56.7 3.0 add_convert_fusion.1
  66.0 67.0 %psum.58 = f32[16,32]{1,0:T(8,128)S(1)} all-reduce(f32[16,32]{1,0:T(8,128)S(1)} %convert_reduce_fusion.1), channel_id=1, replica_groups=mesh['row'=16,'col'=32] {'col'}, use_global_device_ids=true, to_apply=%region_3.4 | all-reduce | flops 512 | bytes 4096 | tf_op jit(solution)/shard_map/psum | solution.py:121
  133.0 41.1 %psum.59 = f32[16,32]{1,0:T(8,128)S(1)} all-reduce(f32[16,32]{1,0:T(8,128)S(1)} %psum.58), channel_id=1, replica_groups=mesh['row'=16,'col'=32] {'row'}, use_global_device_ids=true, to_apply=%region_4.5 | all-reduce | flops 512 | bytes 4096 | tf_op jit(solution)/shard_map/psum | solution.py:121
  174.3 5.4 fusion.26
  179.7 276.1 %all-reduce.5.cloned.1.call-done = f32[16,32,32]{1,2,0:T(8,128)} async-done(((f32[16,32,32]{1,2,0:T(8,128)}), f32[16,32,32]{1,2,0:T(8,128)}) %all-reduce.5.cloned.1.call-update) | async-done | bytes 65552 | tf_op jit(solution)/shard_map/psum | solution.py:121
  455.8 150.4 %all-reduce.7.cloned.1.call-done = f32[16,32,32]{1,2,0:T(8,128)} async-done(((f32[16,32,32]{1,2,0:T(8,128)}), f32[16,32,32]{1,2,0:T(8,128)}) %all-reduce.7.cloned.1.call-update) | async-done | bytes 65552 | tf_op jit(solution)/shard_map/psum | solution.py:121
  606.2 6.1 fusion.1
  617.9 2.6 collective-permute-start.9
  620.7 2.9 collective-permute-done.9
  623.6 4.4 collective-permute-start.10
  629.4 4.8 collective-permute-done.11
  636.5 2.7 collective-permute-start.12
  642.8 2.3 collective-permute-done.13
  645.2 5.5 collective-permute-start.14
  654.1 2.8 collective-permute-done.15
  657.2 3.0 add_convert_fusion
  666.5 62.0 %psum.62 = f32[16,32]{1,0:T(8,128)S(1)} all-reduce(f32[16,32]{1,0:T(8,128)S(1)} %convert_reduce_fusion), channel_id=1, replica_groups=mesh['row'=16,'col'=32] {'col'}, use_global_device_ids=true, to_apply=%region_8.9 | all-reduce | flops 512 | bytes 4096 | tf_op jit(solution)/shard_map/psum | solution.py:121
  728.5 41.4 %psum.63 = f32[16,32]{1,0:T(8,128)S(1)} all-reduce(f32[16,32]{1,0:T(8,128)S(1)} %psum.62), channel_id=1, replica_groups=mesh['row'=16,'col'=32] {'row'}, use_global_device_ids=true, to_apply=%region_9.10 | all-reduce | flops 512 | bytes 4096 | tf_op jit(solution)/shard_map/psum | solution.py:121
  770.2 5.4 fusion.29
  775.6 278.1 %all-reduce.9.cloned.1.call-done = f32[16,32,32]{1,2,0:T(8,128)} async-done(((f32[16,32,32]{1,2,0:T(8,128)}), f32[16,32,32]{1,2,0:T(8,128)}) %all-reduce.9.cloned.1.call-update) | async-done | bytes 65552 | tf_op jit(solution)/shard_map/psum | solution.py:121
  1053.7 150.3 %all-reduce.11.cloned.1.call-done = f32[16,32,32]{1,2,0:T(8,128)} async-done(((f32[16,32,32]{1,2,0:T(8,128)}), f32[16,32,32]{1,2,0:T(8,128)}) %all-reduce.11.cloned.1.call-update) | async-done | bytes 65552 | tf_op jit(solution)/shard_map/psum | solution.py:121
  1204.0 6.1 fusion
  1214.4 2.6 collective-permute-start.17
  1217.3 2.2 collective-permute-done.17
  1219.5 4.4 collective-permute-start.18
  1225.6 4.2 collective-permute-done.19
  (191 shorter events, 59.7 us)
Async XLA Ops:
  7.2 14.3 %copy-start.14 = (f32[2,3,3,1024]{3,0,2,1:T(2,128)S(1)}, f32[2,3,3,1024]{3,0,2,1:T(2,128)}, u32[]{:S(2)}) copy-start(f32[2,3,3,1024]{3,0,2,1:T(2,128)} %param.17) | copy-start | bytes 221188
  7.2 14.4 %copy-start.9 = (f32[2,5,5,768]{3,0,2,1:T(2,128)S(1)}, f32[2,5,5,768]{3,0,2,1:T(2,128)}, u32[]{:S(2)}) copy-start(f32[2,5,5,768]{3,0,2,1:T(2,128)} %param.22) | copy-start | bytes 460804
  7.2 448.5 %all-reduce.5.cloned.1.call-start = ((), (), s32[]{:S(2)}) async-start(), calls=%async_computation | async-start | bytes 524288 | tf_op jit(solution)/shard_map/psum | solution.py:121
  8.6 13.8 %copy-start.36 = (f32[2,256]{1,0:T(2,128)S(1)}, f32[2,256]{1,0:T(2,128)}, u32[]{:S(2)}) copy-start(f32[2,256]{1,0:T(2,128)} %param.25) | copy-start | bytes 6148
  10.1 12.8 %collective-permute-start = (bf16[1,32,1024]{2,1,0:T(8,128)(2,1)S(1)}, bf16[1,32,1024]{2,1,0:T(8,128)(2,1)S(1)}, u32[]{:S(2)}, u32[]{:S(2)}) collective-permute-start(bf16[1,32,1024]{2,1,0:T(8,128)(2,1)S(1)} %get-tuple-element.74), channel_id=1, source_target_pairs={{0,32},{32,64},{64,96},{96,128},{128,160},{160,192},{192,224},{224... | collective-permute-start | bytes 196616 | tf_op jit(solution)/shard_map/ppermute | solution.py:17
  14.7 8.2 collective-permute-start.1
  23.1 3.9 collective-permute-start.2
  24.9 6.3 collective-permute-start.3
  34.1 7.9 collective-permute-start.4
  37.8 6.1 collective-permute-start.5
  44.0 9.3 collective-permute-start.6
  50.0 6.2 collective-permute-start.7
  174.1 432.1 %all-reduce.7.cloned.1.call-start = ((), (), s32[]{:S(2)}) async-start(), calls=%async_computation.1 | async-start | bytes 524288 | tf_op jit(solution)/shard_map/psum | solution.py:121
  455.8 597.9 %all-reduce.9.cloned.1.call-start = ((), (), s32[]{:S(2)}) async-start(), calls=%async_computation.2 | async-start | bytes 524288 | tf_op jit(solution)/shard_map/psum | solution.py:121
  616.0 4.6 collective-permute-start.8
  617.9 5.6 collective-permute-start.9
  620.6 13.9 %copy-start.33 = (f32[1,1024]{1,0:T(1,128)S(1)}, f32[1,1024]{1,0:T(1,128)}, u32[]{:S(2)}) copy-start(f32[1,1024]{1,0:T(1,128)} %get-tuple-element.108) | copy-start | bytes 12292
  620.6 13.9 %copy-start.38 = (f32[1,256]{1,0:T(1,128)S(1)}, f32[1,256]{1,0:T(1,128)}, u32[]{:S(2)}) copy-start(f32[1,256]{1,0:T(1,128)} %get-tuple-element.114) | copy-start | bytes 3076
  620.6 13.9 %copy-start.43 = (bf16[2,1024,256]{2,1,0:T(8,128)(2,1)S(1)}, bf16[2,1024,256]{2,1,0:T(8,128)(2,1)}, u32[]{:S(2)}) copy-start(bf16[2,1024,256]{2,1,0:T(8,128)(2,1)} %param.19) | copy-start | bytes 3145732
  623.6 5.8 collective-permute-start.10
  628.0 6.3 collective-permute-start.11
  636.5 6.3 collective-permute-start.12
  639.2 5.9 collective-permute-start.13
  645.2 9.0 collective-permute-start.14
  650.7 6.2 collective-permute-start.15
  769.9 434.1 %all-reduce.11.cloned.1.call-start = ((), (), s32[]{:S(2)}) async-start(), calls=%async_computation.3 | async-start | bytes 524288 | tf_op jit(solution)/shard_map/psum | solution.py:121
  1212.2 18.6 %copy-start.46 = (f32[4]{0:T(128)S(1)}, f32[4]{0:T(128)}, u32[]{:S(2)}) copy-start(f32[4]{0:T(128)} %param.27) | copy-start | bytes 52
  1212.5 19.2 %copy-start.4 = (bf16[8,32,256]{2,1,0:T(8,128)(2,1)}, bf16[8,32,256]{2,1,0:T(8,128)(2,1)S(1)}, u32[]{:S(2)}) copy-start(bf16[8,32,256]{2,1,0:T(8,128)(2,1)S(1)} %fusion.9) | copy-start | bytes 393220
  1212.5 4.8 collective-permute-start.16
  1214.4 5.1 collective-permute-start.17
  1219.5 6.0 collective-permute-start.18
  1223.9 5.9 collective-permute-start.19
  (39 other events, 159.4 us)
Sparse Core Ops, SparseCore 0:
  174.2 281.4 all-reduce.4
  458.9 147.2 all-reduce.6
  770.1 283.6 all-reduce.8
  1056.7 147.2 all-reduce.10
